TPU v7x, 32 devices: a whole 2x2x4 slice. The times are simulated.
32 devices in a mesh: dp: 8 (over y, x, core), tensor: 4 (over z).
Axes of the slice: x: 2, y: 2, z: 4, core: 2. Of those that a mesh axis runs over, the one named last changes fastest.
Arguments:
- features: float32 [1024, 16, 100], P('tensor', 'dp'), may hold values from -40 to 40
- table_ids: int32 [1024, 16], P(None, 'dp'), may hold values from 0 to 4, as said below
- train_flags: int32 [1024, 16], P(None, 'dp'), may hold values from 0 to 1, as said below
- enc_w: bfloat16 [100, 512], replicated, may hold values from -0.625 to 0.625
- enc_b: float32 [512], replicated, may hold values from -3 to 3
- w_qkv: bfloat16 [2, 3, 512, 512], P(None, None, None, 'tensor'), may hold values from -0.25 to 0.25
- b_qv: float32 [2, 2, 512], P(None, None, 'tensor'), may hold values from -3 to 3
- w_out: bfloat16 [2, 512, 512], P(None, 'tensor'), may hold values from -1 to 1
- out_bias: float32 [2, 2, 512], replicated, may hold values from -2 to 2
- ln_gain: float32 [2, 2, 512], replicated, may hold values from 0.5 to 1.5
- ln_bias: float32 [2, 2, 512], replicated, may hold values from -2 to 2
- w_up: bfloat16 [2, 512, 1024], P(None, None, 'tensor'), may hold values from -0.25 to 0.25
- b_up: float32 [2, 1024], P(None, 'tensor'), may hold values from -3 to 3
- w_down: bfloat16 [2, 1024, 512], P(None, 'tensor'), may hold values from -0.1875 to 0.1875
- cotangent: bfloat16 [1024, 16, 512], P('tensor', 'dp'), may hold values from -6 to 6
Outputs:
- final_rows: bfloat16 [1024, 16, 512], P('tensor', 'dp')
- grad_features: float32 [1024, 16, 100], P('tensor', 'dp')
- grad_enc_w: float32 [100, 512], replicated
- grad_enc_b: float32 [512], replicated
- grad_w_qkv: float32 [2, 3, 512, 512], P(None, None, None, 'tensor')
- grad_b_qv: float32 [2, 2, 512], P(None, None, 'tensor')
- grad_w_out: float32 [2, 512, 512], P(None, 'tensor')
- grad_out_bias: float32 [2, 2, 512], replicated
- grad_ln_gain: float32 [2, 2, 512], replicated
- grad_ln_bias: float32 [2, 2, 512], replicated
- grad_w_up: float32 [2, 512, 1024], P(None, None, 'tensor')
- grad_b_up: float32 [2, 1024], P(None, 'tensor')
- grad_w_down: float32 [2, 1024, 512], P(None, 'tensor')
Inputs may be any that keep to these rules, and one draw needn't show every extreme that they name: `table_ids`: along the rows of a sequence the table ids never fall, and all 5 tables occur in every sequence. `train_flags`: the first row of every table is a train row.
All inputs are finite; a program needn't handle non-finite values.
Results may differ from a plain program's by a relative error of at most 0.03.
Values may be sent and summed in bfloat16 or wider, within the bound.
No kernel may reach another device: no remote copies, remote signals or barrier semaphores. Data moves between devices by JAX's collectives and lax.ppermute only.
A program may use at most 128 MiB of HBM per device.

v0:
```python
import math

import jax
import jax.numpy as jnp
from jax import lax
from jax.sharding import PartitionSpec as P

HD = 128
NTAB = 5


spread_floor = 0.1
norm_eps = 1e-05
highest = lax.Precision.HIGHEST


def layer_norm(values, norm_gain, norm_shift):
    centre = values - jnp.mean(values, -1, keepdims=True)
    spread = jnp.mean(centre * centre, -1, keepdims=True)
    return centre * lax.rsqrt(spread + norm_eps) * norm_gain + norm_shift


def gelu_exact(values):
    return jax.nn.gelu(values, approximate=False)


def gather_rows(values):
    return lax.all_gather(values, "tensor", axis=0, tiled=True)


def gather_grads(values):
    return lax.all_gather(values, "tensor", axis=0, tiled=True)


def scatter_rows(values, weight, pattern, part_rows):

    def row_term(offset, length):
        return jnp.einsum(pattern, values, weight, preferred_element_type=jnp.float32)

    return lax.psum_scatter(
        row_term(jnp.int32(0), part_rows * lax.axis_size("tensor")),
        "tensor",
        scatter_dimension=0,
        tiled=True,
    )


def scatter_grads(values, weight, pattern, part_rows):

    def row_term(offset, length):
        return jnp.einsum(pattern, values, weight, preferred_element_type=jnp.float32)

    return lax.psum_scatter(
        row_term(jnp.int32(0), part_rows * lax.axis_size("tensor")),
        "tensor",
        scatter_dimension=0,
        tiled=True,
    )


def allowed_pairs(table_cols, train_cols, offset, block_rows):
    table_block = lax.dynamic_slice_in_dim(table_cols, offset, block_rows, 1)
    return (table_block[:, None, :, None] == table_cols[:, None, None, :]) & (
        train_cols[:, None, None, :] > 0
    )


def attend(head_parts, table_cols, train_cols, block_rows):
    q_heads, k_heads, v_heads = head_parts
    scaling = 1.0 / math.sqrt(q_heads.shape[3])

    def one_block(block_index):
        offset = block_index * block_rows
        q_block = lax.dynamic_slice_in_dim(q_heads, offset, block_rows, 0)
        allowed = allowed_pairs(table_cols, train_cols, offset, block_rows)
        scores = (
            jnp.einsum("qshd,kshd->shqk", q_block, k_heads, preferred_element_type=jnp.float32)
            * scaling
        )
        scores = jnp.where(allowed, scores, -1e30)
        ceiling = jnp.max(scores, -1, keepdims=True)
        weights = jnp.where(allowed, jnp.exp(scores - ceiling), 0.0)
        totals = jnp.sum(weights, -1, keepdims=True)
        weights_low = (weights / totals).astype(jnp.bfloat16)
        mixture = jnp.einsum(
            "shqk,kshd->qshd", weights_low, v_heads, preferred_element_type=jnp.float32
        )
        return (mixture, ceiling[..., 0] + jnp.log(totals[..., 0]))

    mixture, log_total = lax.map(one_block, jnp.arange(q_heads.shape[0] // block_rows))
    return (mixture.reshape(q_heads.shape), log_total)


def attend_back(head_parts, grad_heads, log_total, table_cols, train_cols, block_rows):
    q_heads, k_heads, v_heads = head_parts
    scaling = 1.0 / math.sqrt(q_heads.shape[3])

    def one_block(carry, block_item):
        grad_keys, grad_values = carry
        block_index, log_block = block_item
        offset = block_index * block_rows
        q_block = lax.dynamic_slice_in_dim(q_heads, offset, block_rows, 0)
        g_block = lax.dynamic_slice_in_dim(grad_heads, offset, block_rows, 0)
        allowed = allowed_pairs(table_cols, train_cols, offset, block_rows)
        scores = (
            jnp.einsum("qshd,kshd->shqk", q_block, k_heads, preferred_element_type=jnp.float32)
            * scaling
        )
        weights = jnp.where(
            allowed, jnp.exp(jnp.where(allowed, scores, 0.0) - log_block[..., None]), 0.0
        )
        grad_weights = jnp.einsum(
            "qshd,kshd->shqk", g_block, v_heads, preferred_element_type=jnp.float32
        )
        grad_scores = weights * (grad_weights - jnp.sum(weights * grad_weights, -1, keepdims=True))
        grad_low = grad_scores.astype(jnp.bfloat16)
        grad_query = (
            jnp.einsum("shqk,kshd->qshd", grad_low, k_heads, preferred_element_type=jnp.float32)
            * scaling
        )
        grad_keys = (
            grad_keys
            + jnp.einsum("shqk,qshd->kshd", grad_low, q_block, preferred_element_type=jnp.float32)
            * scaling
        )
        grad_values = grad_values + jnp.einsum(
            "shqk,qshd->kshd",
            weights.astype(jnp.bfloat16),
            g_block,
            preferred_element_type=jnp.float32,
        )
        return ((grad_keys, grad_values), grad_query)

    empty = jnp.zeros(k_heads.shape, jnp.float32)
    blocks = q_heads.shape[0] // block_rows
    (grad_keys, grad_values), grad_query = lax.scan(
        one_block, (empty, empty), (jnp.arange(blocks), log_total)
    )
    return (grad_query.reshape(q_heads.shape), grad_keys, grad_values)


def stack_layers(entries, position):
    return jnp.stack([entry[position] for entry in entries[::-1]])


def local(
    features,
    table_ids,
    train_flags,
    enc_w,
    enc_b,
    w_qkv,
    b_qv,
    w_out,
    out_bias,
    ln_gain,
    ln_bias,
    w_up,
    b_up,
    w_down,
    cotangent,
):
    part_rows = features.shape[0]
    seq_length = table_ids.shape[0]
    block_rows = min(512, seq_length)
    layers = w_qkv.shape[0]
    local_heads = w_qkv.shape[3] // HD
    offset = lax.axis_index("tensor") * part_rows
    tables_own = lax.dynamic_slice_in_dim(table_ids, offset, part_rows, 0)
    train_own = lax.dynamic_slice_in_dim(train_flags, offset, part_rows, 0)
    member = (tables_own[..., None] == jnp.arange(NTAB, dtype=jnp.int32)).astype(jnp.float32)
    picked = member * train_own[..., None].astype(jnp.float32)
    counts, sums_one, sums_two = lax.psum(
        (
            jnp.sum(picked, 0),
            jnp.einsum("rst,rsf->stf", picked, features, precision=highest),
            jnp.einsum("rst,rsf->stf", picked, features * features, precision=highest),
        ),
        "tensor",
    )
    table_means = sums_one / counts[..., None]
    excess = sums_two / counts[..., None] - table_means * table_means
    scales = lax.rsqrt(jnp.maximum(excess, spread_floor))
    mean_rows = jnp.einsum("rst,stf->rsf", member, table_means, precision=highest)
    scale_rows = jnp.einsum("rst,stf->rsf", member, scales, precision=highest)
    centred = features - mean_rows
    normed = (centred * scale_rows).astype(jnp.bfloat16)
    current = jnp.einsum("rsf,fd->rsd", normed, enc_w, preferred_element_type=jnp.float32) + enc_b
    table_cols = table_ids.T
    train_cols = train_flags.T
    saved = []
    for layer_index in range(layers):
        inputs_low = current.astype(jnp.bfloat16)
        full_in = gather_rows(inputs_low)
        projected = jnp.einsum(
            "rsd,cdh->crsh", full_in, w_qkv[layer_index], preferred_element_type=jnp.float32
        )
        queries = (projected[0] + b_qv[layer_index, 0]).astype(jnp.bfloat16)
        key_rows = projected[1].astype(jnp.bfloat16)
        value_rows = (projected[2] + b_qv[layer_index, 1]).astype(jnp.bfloat16)
        head_shape = queries.shape[:2] + (local_heads, HD)
        head_parts = (
            queries.reshape(head_shape),
            key_rows.reshape(head_shape),
            value_rows.reshape(head_shape),
        )
        mixture, log_total = attend(head_parts, table_cols, train_cols, block_rows)
        mixture_low = mixture.reshape(queries.shape).astype(jnp.bfloat16)
        qkv_full, out_full = (w_qkv[layer_index], w_out[layer_index])
        mixture_own = mixture_low
        attention = (
            scatter_rows(mixture_low, w_out[layer_index], "rsh,hd->rsd", part_rows)
            + out_bias[layer_index, 0]
        )
        before_middle = current + attention
        middle = layer_norm(before_middle, ln_gain[layer_index, 0], ln_bias[layer_index, 0])
        middle_low = middle.astype(jnp.bfloat16)
        up_full, down_full, up_bias = (w_up[layer_index], w_down[layer_index], b_up[layer_index])
        middle_rows = gather_rows(middle_low)
        hidden = (
            jnp.einsum("rsd,df->rsf", middle_rows, up_full, preferred_element_type=jnp.float32)
            + up_bias
        )
        activation = gelu_exact(hidden).astype(jnp.bfloat16)
        feedforward = scatter_rows(activation, down_full, "rsf,fd->rsd", part_rows)
        before_out = middle + feedforward + out_bias[layer_index, 1]
        saved.append(
            (
                full_in,
                head_parts,
                log_total,
                mixture_own,
                qkv_full,
                out_full,
                before_middle,
                middle_rows,
                up_full,
                down_full,
                hidden,
                activation,
                before_out,
            )
        )
        current = layer_norm(before_out, ln_gain[layer_index, 1], ln_bias[layer_index, 1])
    final_rows = current.astype(jnp.bfloat16)
    grad_rows = cotangent.astype(jnp.float32)
    sharded_list = []
    shared_list = []
    for layer_index in reversed(range(layers)):
        (
            full_in,
            head_parts,
            log_total,
            mixture_own,
            qkv_full,
            out_full,
            before_middle,
            middle_rows,
            up_full,
            down_full,
            hidden,
            activation,
            before_out,
        ) = saved[layer_index]
        pullback = jax.vjp(
            layer_norm, before_out, ln_gain[layer_index, 1], ln_bias[layer_index, 1]
        )[1]
        grad_before_out, gain_out, shift_out = pullback(grad_rows)
        grad_ffn = grad_before_out.astype(jnp.bfloat16)
        grad_ffn_rows = gather_grads(grad_ffn)
        grad_down = jnp.einsum(
            "rsf,rsd->fd", activation, grad_ffn_rows, preferred_element_type=jnp.float32
        )
        grad_act = jnp.einsum(
            "rsd,fd->rsf", grad_ffn_rows, down_full, preferred_element_type=jnp.float32
        )
        grad_hidden = jax.vjp(gelu_exact, hidden)[1](grad_act)[0].astype(jnp.bfloat16)
        grad_up_bias = jnp.sum(grad_hidden.astype(jnp.float32), (0, 1))
        grad_up = jnp.einsum(
            "rsd,rsf->df", middle_rows, grad_hidden, preferred_element_type=jnp.float32
        )
        grad_back = scatter_grads(grad_hidden, up_full, "rsf,df->rsd", part_rows)
        grad_middle = grad_before_out + grad_back
        pullback = jax.vjp(
            layer_norm, before_middle, ln_gain[layer_index, 0], ln_bias[layer_index, 0]
        )[1]
        grad_before_middle, gain_middle, shift_middle = pullback(grad_middle)
        grad_attn = grad_before_middle.astype(jnp.bfloat16)
        grad_attn_rows = gather_grads(grad_attn)
        grad_out_w = jnp.einsum(
            "rsh,rsd->hd", mixture_own, grad_attn_rows, preferred_element_type=jnp.float32
        )
        grad_mixture = jnp.einsum(
            "rsd,hd->rsh", grad_attn_rows, out_full, preferred_element_type=jnp.float32
        ).astype(jnp.bfloat16)
        grad_heads = attend_back(
            head_parts,
            grad_mixture.reshape(head_parts[0].shape),
            log_total,
            table_cols,
            train_cols,
            block_rows,
        )
        grad_proj = jnp.stack(
            [
                grad_part.reshape(grad_mixture.shape).astype(jnp.bfloat16)
                for grad_part in grad_heads
            ],
            2,
        )
        grad_qkv = jnp.einsum(
            "rsd,rsch->cdh", full_in, grad_proj, preferred_element_type=jnp.float32
        )
        grad_bias_qv = jnp.stack(
            [
                jnp.sum(grad_proj[:, :, 0].astype(jnp.float32), (0, 1)),
                jnp.sum(grad_proj[:, :, 2].astype(jnp.float32), (0, 1)),
            ]
        )
        grad_rows = grad_before_middle + scatter_grads(
            grad_proj, qkv_full, "rsch,cdh->rsd", part_rows
        )
        gains = jnp.stack([gain_middle, gain_out])
        shifts = jnp.stack([shift_middle, shift_out])
        biases = jnp.stack(
            [
                jnp.sum(grad_attn.astype(jnp.float32), (0, 1)),
                jnp.sum(grad_ffn.astype(jnp.float32), (0, 1)),
            ]
        )
        sharded_list.append((grad_qkv, grad_bias_qv, grad_out_w, grad_up, grad_up_bias, grad_down))
        shared_list.append((gains, shifts, biases))
    grad_low = grad_rows.astype(jnp.bfloat16)
    grad_enc_b = jnp.sum(grad_low.astype(jnp.float32), (0, 1))
    grad_enc_w = jnp.einsum("rsf,rsd->fd", normed, grad_low, preferred_element_type=jnp.float32)
    grad_normed = jnp.einsum("rsd,fd->rsf", grad_low, enc_w, preferred_element_type=jnp.float32)
    sum_plain, sum_centred = lax.psum(
        (
            jnp.einsum("rst,rsf->stf", member, grad_normed, precision=highest),
            jnp.einsum("rst,rsf->stf", member, grad_normed * centred, precision=highest),
        ),
        "tensor",
    )
    grad_excess = jnp.where(
        excess > spread_floor, -0.5 * scales * scales * scales * sum_centred, 0.0
    )
    grad_means = -scales * sum_plain - 2.0 * table_means * grad_excess
    grad_features = (
        grad_normed * scale_rows
        + jnp.einsum("rst,stf->rsf", picked, grad_means / counts[..., None], precision=highest)
        + 2.0
        * features
        * jnp.einsum("rst,stf->rsf", picked, grad_excess / counts[..., None], precision=highest)
    )
    grad_qkv_all, grad_bqv_all, grad_out_all, grad_up_all, grad_upb_all, grad_down_all = lax.psum(
        (
            stack_layers(sharded_list, 0),
            stack_layers(sharded_list, 1),
            stack_layers(sharded_list, 2),
            stack_layers(sharded_list, 3),
            stack_layers(sharded_list, 4),
            stack_layers(sharded_list, 5),
        ),
        "dp",
    )
    gain_grads, shift_grads, bias_grads, grad_enc_w, grad_enc_b = lax.psum(
        (
            stack_layers(shared_list, 0),
            stack_layers(shared_list, 1),
            stack_layers(shared_list, 2),
            grad_enc_w,
            grad_enc_b,
        ),
        ("dp", "tensor"),
    )
    return (
        final_rows,
        grad_features,
        grad_enc_w,
        grad_enc_b,
        grad_qkv_all,
        grad_bqv_all,
        grad_out_all,
        bias_grads,
        gain_grads,
        shift_grads,
        grad_up_all,
        grad_upb_all,
        grad_down_all,
    )


def solution(mesh):
    in_specs = (
        P("tensor", "dp", None),
        P(None, "dp"),
        P(None, "dp"),
        P(),
        P(),
        P(None, None, None, "tensor"),
        P(None, None, "tensor"),
        P(None, "tensor", None),
        P(),
        P(),
        P(),
        P(None, None, "tensor"),
        P(None, "tensor"),
        P(None, "tensor", None),
        P("tensor", "dp", None),
    )
    out_specs = (
        P("tensor", "dp", None),
        P("tensor", "dp", None),
        P(),
        P(),
        P(None, None, None, "tensor"),
        P(None, None, "tensor"),
        P(None, "tensor", None),
        P(),
        P(),
        P(),
        P(None, None, "tensor"),
        P(None, "tensor"),
        P(None, "tensor", None),
    )
    return jax.shard_map(local, mesh=mesh, in_specs=in_specs, out_specs=out_specs, check_vma=False)
```

profile of v0, /device:TPU:1, one launch (start us, length us, event | category | flops | bytes accessed | tf_op | source)
XLA Modules:
  0.0 1417.6 jit_solution(10969170013339509002)
XLA Ops:
  10.8 16.3 %all-reduce.4 = (f32[2,5,100]{2,1,0:T(8,128)S(1)}, f32[2,5]{1,0:T(2,128)S(1)}, f32[2,5,100]{2,1,0:T(8,128)S(1)}) all-reduce(f32[2,5,100]{2,1,0:T(8,128)S(1)} %fusion.177, f32[2,5]{1,0:T(2,128)S(1)} %select_reduce_fusion, f32[2,5,100]{2,1,0:T(8,128)S(1)} %fusion.173), channel_id=1, replica_groups=mesh['dp'=8,'tensor'=4] {'tensor'}, use_global_device_ids=true, to_apply=%region_0.0 | all-reduce | flops 2010 | bytes 16080 | tf_op jit(solution)/shard_map/psum | solution.py:173
  31.8 47.5 %all-gather.9.cloned.1.call-done = bf16[1024,2,512]{2,0,1:T(8,128)(2,1)} async-done(((bf16[256,2,512]{2,0,1:T(8,128)(2,1)}), bf16[1024,2,512]{2,0,1:T(8,128)(2,1)}) %all-gather.9.cloned.1.call-update) | async-done | bytes 2097168 | tf_op jit(solution)/shard_map/all_gather | solution.py:28
  101.7 73.3 %reduce-scatter.9.cloned.1.call-done = f32[256,2,512]{2,0,1:T(8,128)} async-done(((f32[1024,2,512]{2,0,1:T(8,128)}), f32[256,2,512]{2,0,1:T(8,128)}) %reduce-scatter.9.cloned.1.call-update) | async-done | bytes 1048592 | tf_op jit(solution)/shard_map/reduce_scatter | solution.py:40
  178.5 45.9 %all-gather.11.cloned.1.call-done = bf16[1024,2,512]{2,0,1:T(8,128)(2,1)} async-done(((bf16[256,2,512]{2,0,1:T(8,128)(2,1)}), bf16[1024,2,512]{2,0,1:T(8,128)(2,1)}) %all-gather.11.cloned.1.call-update) | async-done | bytes 2097168 | tf_op jit(solution)/shard_map/all_gather | solution.py:28
  236.8 75.7 %reduce-scatter.11.cloned.1.call-done = f32[256,2,512]{2,0,1:T(8,128)} async-done(((f32[1024,2,512]{2,0,1:T(8,128)}), f32[256,2,512]{2,0,1:T(8,128)}) %reduce-scatter.11.cloned.1.call-update) | async-done | bytes 1048592 | tf_op jit(solution)/shard_map/reduce_scatter | solution.py:40
  315.8 46.2 %all-gather.13.cloned.1.call-done = bf16[1024,2,512]{2,0,1:T(8,128)(2,1)} async-done(((bf16[256,2,512]{2,0,1:T(8,128)(2,1)}), bf16[1024,2,512]{2,0,1:T(8,128)(2,1)}) %all-gather.13.cloned.1.call-update) | async-done | bytes 2097168 | tf_op jit(solution)/shard_map/all_gather | solution.py:28
  367.3 17.6 %while.55 = (s32[]{:T(128)}, bf16[2,512,2,1,128]{4,1,0,2,3:T(8,128)(2,1)}, f32[2,2,1,512]{3,1,2,0:T(2,128)S(1)}, s32[2]{0:T(128)}, s32[2,1024]{1,0:T(2,128)S(1)}...) while((s32[]{:T(128)}, ...), condition=%wide.region_17.18_spmd, body=%wide.region_14.17_spmd.sunk | while | flops 557843456 | bytes 18710792 | solution.py:90
  389.1 75.7 %reduce-scatter.13.cloned.1.call-done = f32[256,2,512]{2,0,1:T(8,128)} async-done(((f32[1024,2,512]{2,0,1:T(8,128)}), f32[256,2,512]{2,0,1:T(8,128)}) %reduce-scatter.13.cloned.1.call-update) | async-done | bytes 1048592 | tf_op jit(solution)/shard_map/reduce_scatter | solution.py:40
  468.4 46.5 %all-gather.15.cloned.1.call-done = bf16[1024,2,512]{2,0,1:T(8,128)(2,1)} async-done(((bf16[256,2,512]{2,0,1:T(8,128)(2,1)}), bf16[1024,2,512]{2,0,1:T(8,128)(2,1)}) %all-gather.15.cloned.1.call-update) | async-done | bytes 2097168 | tf_op jit(solution)/shard_map/all_gather | solution.py:28
  527.4 75.7 %reduce-scatter.15.cloned.1.call-done = f32[256,2,512]{2,0,1:T(8,128)} async-done(((f32[1024,2,512]{2,0,1:T(8,128)}), f32[256,2,512]{2,0,1:T(8,128)}) %reduce-scatter.15.cloned.1.call-update) | async-done | bytes 1048592 | tf_op jit(solution)/shard_map/reduce_scatter | solution.py:40
  618.7 36.7 %all-gather.17.cloned.1.call-done = bf16[1024,2,512]{2,0,1:T(8,128)(2,1)} async-done(((bf16[256,2,512]{2,0,1:T(8,128)(2,1)}), bf16[1024,2,512]{2,0,1:T(8,128)(2,1)}) %all-gather.17.cloned.1.call-update) | async-done | bytes 2097168 | tf_op jit(solution)/shard_map/all_gather | solution.py:32
  664.0 75.7 %reduce-scatter.17.cloned.1.call-done = f32[256,2,512]{2,0,1:T(8,128)} async-done(((f32[1024,2,512]{2,0,1:T(8,128)}), f32[256,2,512]{2,0,1:T(8,128)}) %reduce-scatter.17.cloned.1.call-update) | async-done | bytes 1048592 | tf_op jit(solution)/shard_map/reduce_scatter | solution.py:53
  746.6 46.5 %all-gather.19.cloned.1.call-done = bf16[1024,2,512]{2,0,1:T(8,128)(2,1)} async-done(((bf16[256,2,512]{2,0,1:T(8,128)(2,1)}), bf16[1024,2,512]{2,0,1:T(8,128)(2,1)}) %all-gather.19.cloned.1.call-update) | async-done | bytes 2097168 | tf_op jit(solution)/shard_map/all_gather | solution.py:32
  797.1 18.9 %while.56 = (s32[]{:T(128)}, f32[1024,2,1,128]{0,3,1,2:T(8,128)S(1)}, f32[1024,2,1,128]{0,3,1,2:T(8,128)}, bf16[2,512,2,1,128]{4,1,2,3,0:T(8,128)(2,1)}, s32[2]{...) while((s32[]{:T(128)}, ...), condition=%wide.region_31.32_spmd.clone, body=%wide.region_29.31_spmd.clone.sunk | while | flops 1356203008 | bytes 57727424 | solution.py:136
  825.2 75.7 %reduce-scatter.19.cloned.1.call-done = f32[256,2,512]{2,0,1:T(8,128)} async-done(((f32[1024,2,512]{2,0,1:T(8,128)}), f32[256,2,512]{2,0,1:T(8,128)}) %reduce-scatter.19.cloned.1.call-update) | async-done | bytes 1048592 | tf_op jit(solution)/shard_map/reduce_scatter | solution.py:53
  904.8 46.5 %all-gather.21.cloned.1.call-done = bf16[1024,2,512]{2,0,1:T(8,128)(2,1)} async-done(((bf16[256,2,512]{2,0,1:T(8,128)(2,1)}), bf16[1024,2,512]{2,0,1:T(8,128)(2,1)}) %all-gather.21.cloned.1.call-update) | async-done | bytes 2097168 | tf_op jit(solution)/shard_map/all_gather | solution.py:32
  959.8 75.7 %reduce-scatter.21.cloned.1.call-done = f32[256,2,512]{2,0,1:T(8,128)} async-done(((f32[1024,2,512]{2,0,1:T(8,128)}), f32[256,2,512]{2,0,1:T(8,128)}) %reduce-scatter.21.cloned.1.call-update) | async-done | bytes 1048592 | tf_op jit(solution)/shard_map/reduce_scatter | solution.py:53
  1052.9 33.5 %all-gather.23.cloned.1.call-done = bf16[1024,2,512]{2,0,1:T(8,128)(2,1)} async-done(((bf16[256,2,512]{2,0,1:T(8,128)(2,1)}), bf16[1024,2,512]{2,0,1:T(8,128)(2,1)}) %all-gather.23.cloned.1.call-update) | async-done | bytes 2097168 | tf_op jit(solution)/shard_map/all_gather | solution.py:32
  1089.6 15.4 %while.57 = (s32[]{:T(128)}, f32[1024,2,1,128]{0,3,1,2:T(8,128)S(1)}, f32[1024,2,1,128]{0,3,1,2:T(8,128)S(1)}, bf16[2,512,2,1,128]{4,1,2,3,0:T(8,128)(2,1)}, s32...) while((s32[]{:T(128)}, ...), condition=%wide.region_40.41_spmd.clone, body=%wide.region_38.40_spmd.clone.sunk | while | flops 1356203008 | bytes 47241580 | solution.py:136
  1136.3 59.1 %all-reduce.10.cloned.1.call-done = (f32[2,3,512,128]{2,3,1,0:T(8,128)}, f32[2,128,512]{2,1,0:T(8,128)}, f32[2,512,256]{2,1,0:T(8,128)}, f32[2,256,512]{2,1,0:T(8,128)}) async-done(((f32[2,3,512,128]{2,3,1,0:T(8,128)}, f32[2,128,512]{2,1,0:T(8,128)}, f32[2,512,256]{2,1,0:T(8,128)}, f32[2,256,512]{2,1,0:T(8,128)}), (f32[2,3,512,128]{2,3,1,0:T(8,128)}, f32[2,128,512]{2,1,0:T(8,128)}, ...) | async-done | bytes 4194320 | tf_op jit(solution)/shard_map/psum | solution.py:355
  1198.5 76.0 %reduce-scatter.23.cloned.1.call-done = f32[256,2,512]{2,0,1:T(8,128)} async-done(((f32[1024,2,512]{2,0,1:T(8,128)}), f32[256,2,512]{2,0,1:T(8,128)}) %reduce-scatter.23.cloned.1.call-update) | async-done | bytes 1048592 | tf_op jit(solution)/shard_map/reduce_scatter | solution.py:53
  1277.7 14.4 %all-reduce.3 = (f32[2,5,100]{2,1,0:T(8,128)S(1)}, f32[2,5,100]{2,1,0:T(8,128)S(1)}) all-reduce(f32[2,5,100]{2,1,0:T(8,128)S(1)} %fusion.196, f32[2,5,100]{2,1,0:T(8,128)S(1)} %fusion.175), channel_id=1, replica_groups=mesh['dp'=8,'tensor'=4] {'tensor'}, use_global_device_ids=true, to_apply=%region_42.43 | all-reduce | flops 2000 | bytes 16000 | tf_op jit(solution)/shard_map/psum | solution.py:337
  1293.9 41.7 %all-reduce = (f32[512]{0:T(512)}, f32[2,2,512]{2,1,0:T(2,128)}, f32[2,2,512]{2,1,0:T(2,128)}, f32[2,2,512]{2,1,0:T(2,128)}) all-reduce(f32[512]{0:T(512)S(1)} %get-tuple-element.476, f32[2,2,512]{2,1,0:T(2,128)S(1)} %pad_maximum_fusion.10, ...), channel_id=1, replica_groups=mesh['dp'=8,'tensor'=4] {'dp','tensor'}, use_global_device_ids=true, to_apply=%region_46.47 | all-reduce | flops 6656 | bytes 53248 | tf_op jit(solution)/shard_map/psum | solution.py:366
  1335.6 69.3 %all-reduce.8.cloned.1.call-done = f32[100,512]{1,0:T(8,128)} async-done(((f32[100,512]{1,0:T(8,128)}), f32[100,512]{1,0:T(8,128)}) %all-reduce.8.cloned.1.call-update) | async-done | bytes 204816 | tf_op jit(solution)/shard_map/psum | solution.py:366
  (545 shorter events, 256.0 us)
Async XLA Ops:
  7.2 72.2 %all-gather.9.cloned.1.call-start = ((), (), s32[]{:S(2)}) async-start(), calls=%async_computation.8 | async-start | bytes 2621440 | tf_op jit(solution)/shard_map/all_gather | solution.py:28
  31.2 143.7 %reduce-scatter.9.cloned.1.call-start = ((), (), s32[]{:S(2)}) async-start(), calls=%async_computation.9 | async-start | bytes 5242880 | tf_op jit(solution)/shard_map/reduce_scatter | solution.py:40
  99.3 125.1 %all-gather.11.cloned.1.call-start = ((), (), s32[]{:S(2)}) async-start(), calls=%async_computation.10 | async-start | bytes 2621440 | tf_op jit(solution)/shard_map/all_gather | solution.py:28
  101.1 211.3 %copy-start.98 = (f32[1,1,512]{2,1,0:T(1,128)}, f32[1,1,512]{2,1,0:T(1,128)S(1)}, u32[]{:S(2)}) copy-start(f32[1,1,512]{2,1,0:T(1,128)S(1)} %get-tuple-element.514) | copy-start | bytes 6148
  101.1 363.6 %copy-start.100 = (f32[1,1,512]{2,1,0:T(1,128)}, f32[1,1,512]{2,1,0:T(1,128)S(1)}, u32[]{:S(2)}) copy-start(f32[1,1,512]{2,1,0:T(1,128)S(1)} %get-tuple-element.513) | copy-start | bytes 6148
  176.8 135.7 %copy-start.94 = (f32[256,2]{0,1:T(2,128)}, f32[256,2]{0,1:T(2,128)S(1)}, u32[]{:S(2)}) copy-start(f32[256,2]{0,1:T(2,128)S(1)} %fusion.234) | copy-start | bytes 6148
  177.8 134.6 %reduce-scatter.11.cloned.1.call-start = ((), (), s32[]{:S(2)}) async-start(), calls=%async_computation.11 | async-start | bytes 5242880 | tf_op jit(solution)/shard_map/reduce_scatter | solution.py:40
  236.8 125.3 %all-gather.13.cloned.1.call-start = ((), (), s32[]{:S(2)}) async-start(), calls=%async_computation.12 | async-start | bytes 2621440 | tf_op jit(solution)/shard_map/all_gather | solution.py:28
  314.4 150.3 %copy-start.96 = (f32[256,2]{0,1:T(2,128)}, f32[256,2]{0,1:T(2,128)S(1)}, u32[]{:S(2)}) copy-start(f32[256,2]{0,1:T(2,128)S(1)} %fusion.235) | copy-start | bytes 6148
  315.5 149.2 %reduce-scatter.13.cloned.1.call-start = ((), (), s32[]{:S(2)}) async-start(), calls=%async_computation.13 | async-start | bytes 5242880 | tf_op jit(solution)/shard_map/reduce_scatter | solution.py:40
  389.0 125.9 %all-gather.15.cloned.1.call-start = ((), (), s32[]{:S(2)}) async-start(), calls=%async_computation.14 | async-start | bytes 2621440 | tf_op jit(solution)/shard_map/all_gather | solution.py:28
  468.4 134.7 %reduce-scatter.15.cloned.1.call-start = ((), (), s32[]{:S(2)}) async-start(), calls=%async_computation.15 | async-start | bytes 5242880 | tf_op jit(solution)/shard_map/reduce_scatter | solution.py:40
  527.4 128.0 %all-gather.17.cloned.1.call-start = ((), (), s32[]{:S(2)}) async-start(), calls=%async_computation.16 | async-start | bytes 2621440 | tf_op jit(solution)/shard_map/all_gather | solution.py:32
  608.9 130.8 %reduce-scatter.17.cloned.1.call-start = ((), (), s32[]{:S(2)}) async-start(), calls=%async_computation.17 | async-start | bytes 5242880 | tf_op jit(solution)/shard_map/reduce_scatter | solution.py:53
  663.9 129.1 %all-gather.19.cloned.1.call-start = ((), (), s32[]{:S(2)}) async-start(), calls=%async_computation.18 | async-start | bytes 2621440 | tf_op jit(solution)/shard_map/all_gather | solution.py:32
  746.5 154.4 %reduce-scatter.19.cloned.1.call-start = ((), (), s32[]{:S(2)}) async-start(), calls=%async_computation.19 | async-start | bytes 5242880 | tf_op jit(solution)/shard_map/reduce_scatter | solution.py:53
  825.2 126.1 %all-gather.21.cloned.1.call-start = ((), (), s32[]{:S(2)}) async-start(), calls=%async_computation.20 | async-start | bytes 2621440 | tf_op jit(solution)/shard_map/all_gather | solution.py:32
  904.8 130.7 %reduce-scatter.21.cloned.1.call-start = ((), (), s32[]{:S(2)}) async-start(), calls=%async_computation.21 | async-start | bytes 5242880 | tf_op jit(solution)/shard_map/reduce_scatter | solution.py:53
  959.8 126.7 %all-gather.23.cloned.1.call-start = ((), (), s32[]{:S(2)}) async-start(), calls=%async_computation.22 | async-start | bytes 2621440 | tf_op jit(solution)/shard_map/all_gather | solution.py:32
  1040.1 155.3 %all-reduce.10.cloned.1.call-start = ((), (), s32[]{:S(2)}) async-start(), calls=%async_computation.25 | async-start | bytes 8388608 | tf_op jit(solution)/shard_map/psum | solution.py:355
  1114.2 160.3 %reduce-scatter.23.cloned.1.call-start = ((), (), s32[]{:S(2)}) async-start(), calls=%async_computation.23 | async-start | bytes 5242880 | tf_op jit(solution)/shard_map/reduce_scatter | solution.py:53
  1119.0 285.9 %all-reduce.8.cloned.1.call-start = ((), (), s32[]{:S(2)}) async-start(), calls=%async_computation.24 | async-start | bytes 425984 | tf_op jit(solution)/shard_map/psum | solution.py:366
  1122.2 152.2 %copy-start.17 = (f32[256,2,512]{2,0,1:T(8,128)S(1)}, f32[256,2,512]{2,0,1:T(8,128)}, u32[]{:S(2)}) copy-start(f32[256,2,512]{2,0,1:T(8,128)} %copy-done.16) | copy-start | bytes 3145732
  1277.2 131.2 %copy-start.59 = (f32[2,512,256]{2,1,0:T(8,128)S(1)}, f32[2,512,256]{2,1,0:T(8,128)}, u32[]{:S(2)}) copy-start(f32[2,512,256]{2,1,0:T(8,128)} %get-tuple-element.1000) | copy-start | bytes 3145732
  (146 other events, 2424.9 us)
Sparse Core Ops, SparseCore 0:
  31.4 47.9 all-gather.8
  99.4 75.5 reduce-scatter.8
  178.0 46.3 all-gather.10
  236.9 75.5 reduce-scatter.10
  315.6 46.3 all-gather.12
  389.1 75.5 reduce-scatter.12
  468.5 46.3 all-gather.14
  527.5 75.5 reduce-scatter.14
  609.0 46.3 all-gather.16
  664.0 75.5 reduce-scatter.16
  746.7 46.3 all-gather.18
  825.3 75.5 reduce-scatter.18
  904.9 46.3 all-gather.20
  959.9 75.5 reduce-scatter.20
  1040.2 46.1 all-gather.22
  1114.3 81.0 all-reduce.9
  1197.5 76.8 reduce-scatter.22
  1281.4 123.4 all-reduce.7
where the time goes:
time: 1430 us; the launch traced here: 1420 us
  waiting for transfers between devices  1080 us (76%)
  matrix products  107 us (7%)
  blocking collectives  85.8 us (6%)
  other arithmetic  59 us (4%)
  local copies, waits for them, and re-layouts  51.3 us (4%)
  between operations  16.1 us (1%)
    reduce_scatter x4, waiting for transfers between devices, scatter_grads(): lax.psum_scatter(row_term(jnp.int32(0), part_rows * lax.axis_size('tensor...  303 us
    reduce_scatter x4, waiting for transfers between devices, scatter_rows(): lax.psum_scatter(row_term(jnp.int32(0), part_rows * lax.axis_size('tensor...  300 us
    all_gather x4, waiting for transfers between devices, gather_rows(): return lax.all_gather(values, 'tensor', axis=0, tiled=True)  186 us
    all_gather x4, waiting for transfers between devices, gather_grads(): return lax.all_gather(values, 'tensor', axis=0, tiled=True)  163 us
    psum x1, waiting for transfers between devices, local(): lax.psum((stack_layers(shared_list, 0), stack_layers(shared_list, 1), sta...  69.3 us
    psum x1, waiting for transfers between devices, local(): lax.psum((stack_layers(sharded_list, 0), stack_layers(sharded_list, 1), s...  59.1 us
    psum x1, blocking collectives, local(): lax.psum((stack_layers(shared_list, 0), stack_layers(shared_list, 1), sta...  41.7 us
  transfers between devices with their start and end apart: 18, of which 18 were waited for; matrix products, arithmetic and copies ran while one was open for 2% of the time, Pallas kernels for 0%

commit v1 on v0

v1 whole, which is shorter than its diff:
```python
import math

import jax
import jax.numpy as jnp
from jax import lax
from jax.sharding import PartitionSpec as P

HD = 128
NTAB = 5
spread_floor = 0.1
norm_eps = 1e-05
highest = lax.Precision.HIGHEST
f32 = jnp.float32
bf16 = jnp.bfloat16


def dot(a, b, dims):
    return lax.dot_general(a, b, (dims, ((), ())), preferred_element_type=f32)


def swap_dp(values, mask):
    size = lax.axis_size("dp")
    return lax.ppermute(values, "dp", [(i, i ^ mask) for i in range(size)])


def swap_z(values, mask):
    size = lax.axis_size("tensor")
    return lax.ppermute(values, "tensor", [(i, i ^ mask) for i in range(size)])


def relay_pairs(step):
    size, width = lax.axis_size("dp"), lax.axis_size("tensor")
    pairs = []
    for i in range(size):
        for z in range(width):
            target = (i - i % 2 + z // 2) * width + 2 * (i % 2) + (step ^ (z & 1))
            pairs.append((i * width + z, target))
    return pairs


def to_sequences(blocks, z):
    odd = (z & 1) == 1
    got = []
    for step in range(2):
        block = jnp.where(odd, blocks[:, 1 - step], blocks[:, step])
        got.append(lax.ppermute(block, ("dp", "tensor"), relay_pairs(step)))
    return jnp.where(odd, jnp.concatenate([got[1], got[0]]), jnp.concatenate(got))


def from_sequences(rows, z):
    part = rows.shape[0] // 2
    odd = (z & 1) == 1
    first, second = rows[:part], rows[part:]
    got = []
    for step in range(2):
        block = jnp.where(odd, second, first) if step == 0 else jnp.where(odd, first, second)
        pairs = [(b, a) for a, b in relay_pairs(step)]
        got.append(lax.ppermute(block, ("dp", "tensor"), pairs))
    return jnp.where(odd, jnp.stack([got[1], got[0]], 1), jnp.stack(got, 1))


def flip_if(values, bit, axis):
    return jnp.where(bit == 1, jnp.flip(values, axis), values)


def pack_local(wq, wo, wu, wd):
    d, f = wq.shape[1], wu.shape[1]
    q = 8
    a = wq.reshape(3, q, d // q, HD).transpose(1, 0, 2, 3).reshape(q, -1, HD)
    b = wo.reshape(q, HD // q, d // HD, HD).transpose(0, 2, 1, 3).reshape(q, -1, HD)
    c = wu.reshape(q, d // q, f // HD, HD).transpose(0, 2, 1, 3).reshape(q, -1, HD)
    e = wd.reshape(q, f // q, d // HD, HD).transpose(0, 2, 1, 3).reshape(q, -1, HD)
    return jnp.concatenate([a, b, c, e], 1)


def unpack_local(pieces, d, f):
    q = 8
    s1 = 3 * d // q
    s2 = s1 + (HD // q) * (d // HD)
    s3 = s2 + (d // q) * (f // HD)
    wq = pieces[:, :s1].reshape(q, 3, d // q, HD).transpose(1, 0, 2, 3).reshape(3, d, HD)
    wo = pieces[:, s1:s2].reshape(q, d // HD, HD // q, HD).transpose(0, 2, 1, 3).reshape(HD, d)
    wu = pieces[:, s2:s3].reshape(q, f // HD, d // q, HD).transpose(0, 2, 1, 3).reshape(d, f)
    wd = pieces[:, s3:].reshape(q, d // HD, f // q, HD).transpose(0, 2, 1, 3).reshape(f, d)
    return wq, wo, wu, wd


def layer_norm_parts(values):
    centre = values - jnp.mean(values, -1, keepdims=True)
    inv = lax.rsqrt(jnp.mean(centre * centre, -1, keepdims=True) + norm_eps)
    return centre * inv, inv


def layer_norm_back(grad, normal, inv, gain):
    e = grad * gain
    return (
        (e - jnp.mean(e, -1, keepdims=True) - normal * jnp.mean(e * normal, -1, keepdims=True)) * inv,
        jnp.sum(grad * normal, 0),
        jnp.sum(grad, 0),
    )


def gelu_exact(values):
    return jax.nn.gelu(values, approximate=False)


def gather_weights(piece, p, o, z):
    width = lax.axis_size("tensor")
    rows = jnp.stack([piece] + [swap_z(piece, k) for k in range(1, width)])
    plane = jnp.stack([rows] + [swap_dp(rows, 2 * r) for r in range(1, 4)])
    whole = jnp.stack([plane, swap_dp(plane, 1)])
    whole = whole.reshape((2,) * 5 + piece.shape)
    for axis, bit in enumerate((p, o >> 1, o & 1, z >> 1, z & 1)):
        whole = flip_if(whole, bit, axis)
    return whole.reshape((8, width) + piece.shape)


def whole_weights(packed, d, f):
    width = packed.shape[1]
    parts = [unpack_local(packed[:, z], d, f) for z in range(width)]
    return (
        jnp.concatenate([e[0] for e in parts], 2),
        jnp.concatenate([e[1] for e in parts], 0),
        jnp.concatenate([e[2] for e in parts], 1),
        jnp.concatenate([e[3] for e in parts], 0),
    )


def pick(values, index):
    return lax.dynamic_index_in_dim(values, index, 0, keepdims=False)


def reduce_grads(packed, shared, p, o, z):
    width = packed.shape[1]
    piece_rows = packed.shape[2]
    flat = packed.reshape(8, width * piece_rows, HD)
    if shared is not None:
        flat = jnp.concatenate([flat, shared], 1)
    halves = flat.reshape((2, 4) + flat.shape[1:]).astype(bf16)
    own = pick(halves, p).astype(f32) + swap_dp(pick(halves, 1 - p), 1).astype(f32)
    own = own.astype(bf16)
    total = pick(own, o).astype(f32)
    for r in range(1, 4):
        total = total + swap_dp(pick(own, o ^ r), 2 * r).astype(f32)
    mask = 8
    while mask < lax.axis_size("dp"):
        total = total + swap_dp(total.astype(bf16), mask).astype(f32)
        mask *= 2
    low = total.astype(bf16)
    quarters = low[: width * piece_rows].reshape(width, piece_rows, HD)
    rest = low[width * piece_rows :]
    share = jnp.concatenate([pick(quarters, z), rest]).astype(f32)
    for k in range(1, width):
        share = share + swap_z(jnp.concatenate([pick(quarters, z ^ k), rest]), k).astype(f32)
    share = share.astype(bf16)
    plane = jnp.stack([share] + [swap_dp(share, 2 * r) for r in range(1, 4)])
    plane = plane.reshape((2, 2) + share.shape)
    plane = flip_if(flip_if(plane, o >> 1, 0), o & 1, 1).reshape((4,) + share.shape)
    whole = flip_if(jnp.stack([plane, swap_dp(plane, 1)]), p, 0)
    whole = whole.reshape((8,) + share.shape)
    return whole[:, :piece_rows].astype(f32), whole[:, piece_rows:].astype(f32)


def local(
    features,
    table_ids,
    train_flags,
    enc_w,
    enc_b,
    w_qkv,
    b_qv,
    w_out,
    out_bias,
    ln_gain,
    ln_bias,
    w_up,
    b_up,
    w_down,
    cotangent,
):
    part = features.shape[0]
    width = lax.axis_size("tensor")
    layers, d = w_qkv.shape[0], w_qkv.shape[2]
    f_part = w_up.shape[2]
    f_all = f_part * width
    heads = d // HD
    half = 2 * part
    di, z = lax.axis_index("dp"), lax.axis_index("tensor")
    p, o = di % 2, (di // 2) % 4
    q = p * 4 + o

    weights = []
    for l in range(layers):
        piece = pick(pack_local(w_qkv[l], w_out[l], w_up[l], w_down[l]), q)
        weights.append(whole_weights(gather_weights(piece, p, o, z), d, f_all // width))
    bias_local = jnp.concatenate([b_qv.reshape(-1, HD), b_up.reshape(-1, HD)])
    bias_all = lax.all_gather(bias_local, "tensor")
    nb = 2 * layers
    bqv_all = bias_all[:, :nb].transpose(1, 0, 2).reshape(layers, 2, d)
    bup_all = bias_all[:, nb:].reshape(width, layers, f_part).transpose(1, 0, 2).reshape(layers, f_all)

    feat_half = to_sequences(features, z)
    cot_half = to_sequences(cotangent, z)
    codes = (table_ids * 2 + train_flags).T
    other_codes = swap_dp(codes, 1)
    seq_codes = pick(jnp.where(p == z // 2, codes, other_codes), z & 1)
    code_own = lax.dynamic_slice_in_dim(seq_codes, p * half, half)
    code_other = lax.dynamic_slice_in_dim(seq_codes, (1 - p) * half, half)
    code_keys = jnp.concatenate([code_own, code_other])
    member = ((code_own >> 1)[:, None] == jnp.arange(NTAB, dtype=jnp.int32)).astype(f32)
    picked = member * (code_own & 1)[:, None].astype(f32)
    feat_other = swap_dp(feat_half, 1)
    feat_all = jnp.concatenate([feat_half, feat_other])
    picked_all = ((code_keys >> 1)[:, None] == jnp.arange(NTAB, dtype=jnp.int32)).astype(f32) * (
        code_keys & 1
    )[:, None].astype(f32)
    counts = jnp.sum(picked_all, 0)[:, None]
    table_means = jnp.einsum("rt,rf->tf", picked_all, feat_all, precision=highest) / counts
    excess = (
        jnp.einsum("rt,rf->tf", picked_all, feat_all * feat_all, precision=highest) / counts
        - table_means * table_means
    )
    scales = lax.rsqrt(jnp.maximum(excess, spread_floor))
    centred = feat_half - jnp.dot(member, table_means, precision=highest)
    scale_rows = jnp.dot(member, scales, precision=highest)
    normed = (centred * scale_rows).astype(bf16)
    current = dot(normed, enc_w, ((1,), (0,))) + enc_b
    allowed = ((code_own >> 1)[:, None] == (code_keys >> 1)[None, :]) & ((code_keys & 1) > 0)[None, :]
    scaling = 1.0 / math.sqrt(HD)

    saved = []
    for l in range(layers):
        wq, wo, wu, wd = weights[l]
        low = current.astype(bf16)
        queries = (dot(low, wq[0], ((1,), (0,))) + bqv_all[l, 0]).astype(bf16)
        keys = dot(low, wq[1], ((1,), (0,))).astype(bf16)
        values = (dot(low, wq[2], ((1,), (0,))) + bqv_all[l, 1]).astype(bf16)
        kv = jnp.concatenate([keys, values], 1)
        kv_all = jnp.concatenate([kv, swap_dp(kv, 1)])
        mixes, probs_all = [], []
        for h in range(heads):
            qh = queries[:, h * HD : (h + 1) * HD]
            kh = kv_all[:, h * HD : (h + 1) * HD]
            vh = kv_all[:, d + h * HD : d + (h + 1) * HD]
            scores = jnp.where(allowed, dot(qh, kh, ((1,), (1,))) * scaling, -1e30)
            e = jnp.exp(scores - jnp.max(scores, -1, keepdims=True))
            probs = e / jnp.sum(e, -1, keepdims=True)
            probs_all.append(probs)
            mixes.append(dot(probs.astype(bf16), vh, ((1,), (0,))))
        mixture = jnp.concatenate(mixes, 1).astype(bf16)
        before_middle = current + dot(mixture, wo, ((1,), (0,))) + out_bias[l, 0]
        n1, inv1 = layer_norm_parts(before_middle)
        middle = n1 * ln_gain[l, 0] + ln_bias[l, 0]
        middle_low = middle.astype(bf16)
        hidden = dot(middle_low, wu, ((1,), (0,))) + bup_all[l]
        act = gelu_exact(hidden).astype(bf16)
        before_out = middle + dot(act, wd, ((1,), (0,))) + out_bias[l, 1]
        n2, inv2 = layer_norm_parts(before_out)
        current = n2 * ln_gain[l, 1] + ln_bias[l, 1]
        saved.append((low, queries, kv_all, probs_all, mixture, n1, inv1, middle_low, hidden, act, n2, inv2))
    final_rows = from_sequences(current.astype(bf16), z)

    grad = cot_half.astype(f32)
    packs, vectors = [None] * layers, [None] * layers
    for l in reversed(range(layers)):
        low, queries, kv_all, probs_all, mixture, n1, inv1, middle_low, hidden, act, n2, inv2 = saved[l]
        wq, wo, wu, wd = weights[l]
        g_before_out, g_gain1, g_shift1 = layer_norm_back(grad, n2, inv2, ln_gain[l, 1])
        g_ffn = g_before_out.astype(bf16)
        d_down = dot(act, g_ffn, ((0,), (0,)))
        g_act = dot(g_ffn, wd, ((1,), (1,)))
        g_hidden = jax.vjp(gelu_exact, hidden)[1](g_act)[0].astype(bf16)
        d_bup = jnp.sum(g_hidden.astype(f32), 0)
        d_up = dot(middle_low, g_hidden, ((0,), (0,)))
        g_middle = g_before_out + dot(g_hidden, wu, ((1,), (1,)))
        g_before_middle, g_gain0, g_shift0 = layer_norm_back(g_middle, n1, inv1, ln_gain[l, 0])
        g_attn = g_before_middle.astype(bf16)
        d_out = dot(mixture, g_attn, ((0,), (0,)))
        g_mix = dot(g_attn, wo, ((1,), (1,))).astype(bf16)
        gq, gk, gv = [], [], []
        for h in range(heads):
            cols = slice(h * HD, (h + 1) * HD)
            kh, vh = kv_all[:, cols], kv_all[:, d + h * HD : d + (h + 1) * HD]
            probs = probs_all[h]
            g_probs = dot(g_mix[:, cols], vh, ((1,), (1,)))
            g_scores = (probs * (g_probs - jnp.sum(probs * g_probs, -1, keepdims=True))).astype(bf16)
            gq.append(dot(g_scores, kh, ((1,), (0,))) * scaling)
            gk.append(dot(g_scores, queries[:, cols], ((0,), (0,))) * scaling)
            gv.append(dot(probs.astype(bf16), g_mix[:, cols], ((0,), (0,))))
        g_queries = jnp.concatenate(gq, 1).astype(bf16)
        g_kv = jnp.concatenate(gk + gv, 1)
        g_kv = (g_kv[:half] + swap_dp(g_kv[half:].astype(bf16), 1).astype(f32)).astype(bf16)
        g_proj = jnp.concatenate([g_queries, g_kv], 1)
        d_qkv = dot(low, g_proj, ((0,), (0,)))
        g_proj_sum = jnp.sum(g_proj.astype(f32), 0)
        d_bqv = jnp.stack([g_proj_sum[:d], g_proj_sum[2 * d :]])
        wcat = jnp.concatenate([wq[0], wq[1], wq[2]], 1)
        grad = g_before_middle + dot(g_proj, wcat, ((1,), (1,)))
        packs[l] = jnp.stack(
            [
                pack_local(
                    jnp.stack([d_qkv[:, c * d + zz * HD : c * d + (zz + 1) * HD] for c in range(3)]),
                    d_out[zz * HD : (zz + 1) * HD],
                    d_up[:, zz * f_part : (zz + 1) * f_part],
                    d_down[zz * f_part : (zz + 1) * f_part],
                )
                for zz in range(width)
            ],
            1,
        ).astype(bf16)
        vectors[l] = jnp.concatenate(
            [
                jnp.stack([g_gain0, g_gain1, g_shift0, g_shift1]),
                jnp.stack([jnp.sum(g_attn.astype(f32), 0), jnp.sum(g_ffn.astype(f32), 0)]),
                d_bqv,
                d_bup.reshape(-1, d),
            ]
        )
    g_low = grad.astype(bf16)
    d_enc_b = jnp.sum(g_low.astype(f32), 0)
    d_enc_w = dot(normed, g_low, ((0,), (0,)))
    g_normed = dot(g_low, enc_w, ((1,), (1,)))
    sums = jnp.concatenate(
        [
            jnp.einsum("rt,rf->tf", member, g_normed, precision=highest),
            jnp.einsum("rt,rf->tf", member, g_normed * centred, precision=highest),
        ]
    )
    sums = sums + swap_dp(sums, 1)
    sum_plain, sum_centred = sums[:NTAB], sums[NTAB:]
    g_excess = jnp.where(excess > spread_floor, -0.5 * scales * scales * scales * sum_centred, 0.0)
    g_means = -scales * sum_plain - 2.0 * table_means * g_excess
    g_features = (
        g_normed * scale_rows
        + jnp.dot(picked, g_means / counts, precision=highest)
        + 2.0 * feat_half * jnp.dot(picked, g_excess / counts, precision=highest)
    )
    grad_features = from_sequences(g_features, z)

    per = vectors[0].shape[0]
    rows = jnp.concatenate(vectors + [d_enc_b[None], d_enc_w])
    used = rows.shape[0]
    pad = -used % 16
    shared = jnp.pad(rows, ((0, pad), (0, 0))).reshape(8, -1, HD)
    outs = [None] * layers
    for l in reversed(range(layers)):
        pieces, rest = reduce_grads(packs[l], shared if l == 0 else None, p, o, z)
        outs[l] = unpack_local(pieces, d, f_part)
    rows = rest.reshape(used + pad, d)[:used]
    vec = rows[: layers * per].reshape(layers, per, d)
    d_bqv = lax.dynamic_slice_in_dim(vec[:, 6:8], z * HD, HD, 2)
    d_bup = lax.dynamic_slice_in_dim(vec[:, 8:].reshape(layers, f_all), z * f_part, f_part, 1)
    return (
        final_rows,
        grad_features,
        rows[layers * per + 1 :],
        rows[layers * per],
        jnp.stack([e[0] for e in outs]),
        d_bqv,
        jnp.stack([e[1] for e in outs]),
        vec[:, 4:6],
        vec[:, 0:2],
        vec[:, 2:4],
        jnp.stack([e[2] for e in outs]),
        d_bup,
        jnp.stack([e[3] for e in outs]),
    )


def solution(mesh):
    rows, ids = P("tensor", "dp", None), P(None, "dp")
    qkv, bqv = P(None, None, None, "tensor"), P(None, None, "tensor")
    mid, last = P(None, "tensor", None), P(None, None, "tensor")
    in_specs = (rows, ids, ids, P(), P(), qkv, bqv, mid, P(), P(), P(), last, P(None, "tensor"), mid, rows)
    out_specs = (rows, rows, P(), P(), qkv, bqv, mid, P(), P(), P(), last, P(None, "tensor"), mid)
    return jax.shard_map(local, mesh=mesh, in_specs=in_specs, out_specs=out_specs, check_vma=False)
```

time: 1430 us -> 440 us (0.31)
  waiting for transfers between devices: 1080 us -> 72.5 us
  starting transfers between devices: 11.2 us -> 84.2 us
  blocking collectives: 85.8 us -> 14.4 us
  local copies, waits for them, and re-layouts: 51.3 us -> 110 us
  matrix products: 107 us -> 86.9 us
    reduce_scatter x8 -> x0, waiting for transfers between devices: 603 us -> none  [the longest x4 303 us: scatter_grads(): lax.psum_scatter(row_term(jnp.int32(0), part_rows * lax.axis_size('tensor...]
    all_gather x8 -> x0, waiting for transfers between devices: 349 us -> none  [the longest x4 186 us: gather_rows(): return lax.all_gather(values, 'tensor', axis=0, tiled=True)]
    psum x2 -> x0, waiting for transfers between devices: 128 us -> none  [the longest x1 69.3 us: local(): lax.psum((stack_layers(shared_list, 0), stack_layers(shared_list, 1), sta...]
    psum x4 -> x0, blocking collectives: 85.8 us -> none  [the longest x1 41.7 us: local(): lax.psum((stack_layers(shared_list, 0), stack_layers(shared_list, 1), sta...]
    ppermute x0 -> x51, starting transfers between devices: none -> 84.2 us  [the longest x31 37 us: swap_dp(): return lax.ppermute(values, 'dp', [(i, i ^ mask) for i in range(size)])]
    ppermute x0 -> x51, waiting for transfers between devices: none -> 72.5 us  [the longest x31 55.1 us: swap_dp(): return lax.ppermute(values, 'dp', [(i, i ^ mask) for i in range(size)])]
    reshape x0 -> x55, local copies, waits for them, and re-layouts: none -> 32.6 us  [the longest x16 11.5 us: pack_local(): wu.reshape(q, d // q, f // HD, HD).transpose(0, 2, 1, 3).reshape(q, -1, HD)]
    reduce_sum x29 -> x20, other arithmetic: 35.5 us -> 11.6 us  [the longest x8 4.06 us: local(): probs = e / jnp.sum(e, -1, keepdims=True)]
  transfers between devices with their start and end apart: 18 -> 51, of which waited for: 18 -> 14; matrix products, arithmetic and copies ran while one was open for 2% -> 47% of each run, Pallas kernels for 0% -> 0%
where the time goes in v1:
time: 440 us; the launch traced here: 432 us
  local copies, waits for them, and re-layouts  110 us (25%)
  matrix products  86.9 us (20%)
  starting transfers between devices  84.2 us (19%)
  waiting for transfers between devices  72.5 us (16%)
  other arithmetic  58.9 us (13%)
  blocking collectives  14.4 us (3%)
  between operations  5.1 us (1%)
    dot_general x79, matrix products, dot(): return lax.dot_general(a, b, (dims, ((), ())), preferred_element_type=f32)  82.7 us
    ppermute x31, waiting for transfers between devices, swap_dp(): return lax.ppermute(values, 'dp', [(i, i ^ mask) for i in range(size)])  55.1 us
    ppermute x31, starting transfers between devices, swap_dp(): return lax.ppermute(values, 'dp', [(i, i ^ mask) for i in range(size)])  37 us
    unnamed x434, local copies, waits for them, and re-layouts  27.8 us
    ppermute x4, starting transfers between devices, to_sequences(): got.append(lax.ppermute(block, ('dp', 'tensor'), relay_pairs(step)))  17.3 us
    ppermute x12, starting transfers between devices, swap_z(): return lax.ppermute(values, 'tensor', [(i, i ^ mask) for i in range(size)])  16 us
    all_gather x1, blocking collectives, local(): bias_all = lax.all_gather(bias_local, 'tensor')  14.4 us
    ppermute x4, starting transfers between devices, from_sequences(): got.append(lax.ppermute(block, ('dp', 'tensor'), pairs))  13.9 us
  transfers between devices with their start and end apart: 51, of which 14 were waited for; matrix products, arithmetic and copies ran while one was open for 47% of the time, Pallas kernels for 0%

profile of v1, /device:TPU:1, one launch (start us, length us, event | category | flops | bytes accessed | tf_op | source)
XLA Modules:
  0.0 431.9 jit_solution(5051567344120418639)
XLA Ops:
  4.1 4.2 collective-permute-start.6
  10.4 3.5 collective-permute-start.14
  14.6 14.4 %all-gather = f32[32,128]{1,0:T(8,128)S(1)} all-gather(f32[8,128]{1,0:T(8,128)S(1)} %pad_maximum_fusion.44), channel_id=2, replica_groups=mesh['dp'=8,'tensor'=4] {'tensor'}, dimensions={0}, use_global_device_ids=true | all-gather | bytes 20480 | tf_op jit(solution)/shard_map/all_gather | solution.py:197
  39.3 3.2 collective-permute-done.13
  42.4 7.1 %collective-permute-start = (f32[256,100]{0,1:T(8,128)}, f32[256,100]{0,1:T(8,128)S(1)}, u32[]{:S(2)}, u32[]{:S(2)}) collective-permute-start(f32[256,100]{0,1:T(8,128)} %get-tuple-element.211), channel_id=1, source_target_pairs={{0,1},{1,0},{2,5},{3,4},{4,3},{5,2},{6,7},{7,6},{8,9},{9,8},{10,13... | collective-permute-start | bytes 307208 | tf_op jit(solution)/shard_map/ppermute | solution.py:46
  52.4 3.6 collective-permute-done.9
  56.3 8.8 %collective-permute-start.10 = (bf16[4,4,512,128]{3,2,1,0:T(8,128)(2,1)S(1)}, bf16[4,4,512,128]{3,2,1,0:T(8,128)(2,1)S(1)}, u32[]{:S(2)}, u32[]{:S(2)}) collective-permute-start(bf16[4,4,512,128]{3,2,1,0:T(8,128)(2,1)S(1)} %pad_maximum_fusion.4), channel_id=1, source_target_pairs={{0,4},{4,0},{8,12},{12,8},{16,20},{20,16},{24,28},{28,24},{1,5},{5... | collective-permute-start | bytes 6291464 | tf_op jit(solution)/shard_map/ppermute | solution.py:23
  65.4 8.6 %collective-permute-done.16 = bf16[4,512,128]{2,1,0:T(8,128)(2,1)S(1)} collective-permute-done((bf16[4,512,128]{2,1,0:T(8,128)(2,1)S(1)}, bf16[4,512,128]{2,1,0:T(8,128)(2,1)S(1)}, u32[]{:S(2)}, u32[]{:S(2)}) %collective-permute-start.16) | collective-permute-done | bytes 524320 | tf_op jit(solution)/shard_map/ppermute | solution.py:23
  75.9 4.7 %collective-permute-start.23 = (bf16[256,512]{0,1:T(8,128)(2,1)}, bf16[256,512]{0,1:T(8,128)(2,1)S(1)}, u32[]{:S(2)}, u32[]{:S(2)}) collective-permute-start(bf16[256,512]{0,1:T(8,128)(2,1)} %get-tuple-element.193), channel_id=1, source_target_pairs={{0,0},{1,1},{2,4},{3,5},{4,2},{5,3},{6,6},{7,7},{8,8},{9,9},{10,12... | collective-permute-start | bytes 786440 | tf_op jit(solution)/shard_map/ppermute | solution.py:46
  80.6 3.6 collective-permute-start.22
  85.8 3.3 collective-permute-done.3
  124.7 6.8 %multiply_convert_fusion.9 = (bf16[512,1024]{1,0:T(8,128)(2,1)S(1)}, f32[512,1024]{1,0:T(8,128)}, f32[512,1024]{1,0:T(8,128)}) fusion(f32[1024]{0:T(1024)S(1)} %bitcast.884, bf16[512,1024]{1,0:T(8,128)(2,1)S(1)} %bitcast_dynamic-update-slice_fusion.12, f32[512,512]{0,1:T(8,128)S(1)} %get-tuple-element.266, f32[512]{0:T(512)S(1)} %bitcast.890, ...), kind=kOutput, calls=%fused_computation.82 | convolution fusion | flops 572784640 | bytes 7352320 | tf_op jit(solution)/shard_map/dot_general | solution.py:18
  145.8 5.6 %multiply_convert_fusion.8 = (bf16[512,1024]{1,0:T(8,128)(2,1)S(1)}, f32[512,1024]{1,0:T(8,128)S(1)}, f32[512,1024]{1,0:T(8,128)S(1)}) fusion(f32[1024]{0:T(1024)S(1)} %bitcast.886, bf16[512,1024]{1,0:T(8,128)(2,1)S(1)} %bitcast_dynamic-update-slice_fusion.4, f32[512,512]{0,1:T(8,128)S(1)} %get-tuple-element.279, f32[512]{0:T(512)S(1)} %bitcast.894, ...), kind=kOutput, calls=%fused_computation.61 | convolution fusion | flops 572784640 | bytes 7352320 | tf_op jit(solution)/shard_map/dot_general | solution.py:18
  165.0 3.8 collective-permute-start.21
  316.5 7.8 %collective-permute-done.41 = bf16[2048,128]{1,0:T(8,128)(2,1)} collective-permute-done((bf16[2048,128]{1,0:T(8,128)(2,1)}, bf16[2048,128]{1,0:T(8,128)(2,1)}, u32[]{:S(2)}, u32[]{:S(2)}) %collective-permute-start.41) | collective-permute-done | bytes 524320 | tf_op jit(solution)/shard_map/ppermute | solution.py:23
  324.3 12.3 %collective-permute-done.43 = bf16[2048,128]{1,0:T(8,128)(2,1)} collective-permute-done((bf16[2048,128]{1,0:T(8,128)(2,1)}, bf16[2048,128]{1,0:T(8,128)(2,1)}, u32[]{:S(2)}, u32[]{:S(2)}) %collective-permute-start.43) | collective-permute-done | bytes 524320 | tf_op jit(solution)/shard_map/ppermute | solution.py:23
  342.9 3.6 collective-permute-done.46
  346.5 5.2 %collective-permute-done.45 = bf16[512,128]{1,0:T(8,128)(2,1)S(1)} collective-permute-done((bf16[512,128]{1,0:T(8,128)(2,1)S(1)}, bf16[512,128]{1,0:T(8,128)(2,1)S(1)}, u32[]{:S(2)}, u32[]{:S(2)}) %collective-permute-start.45) | collective-permute-done | bytes 131104 | tf_op jit(solution)/shard_map/ppermute | solution.py:28
  359.9 4.7 %collective-permute-start.50 = (bf16[4,512,128]{2,1,0:T(8,128)(2,1)S(1)}, bf16[4,512,128]{2,1,0:T(8,128)(2,1)S(1)}, u32[]{:S(2)}, u32[]{:S(2)}) collective-permute-start(bf16[4,512,128]{2,1,0:T(8,128)(2,1)S(1)} %bitcast.685), channel_id=1, source_target_pairs={{0,4},{4,0},{8,12},{12,8},{16,20},{20,16},{24,28},{28,24},{1,5},{5... | collective-permute-start | bytes 1572872 | tf_op jit(solution)/shard_map/ppermute | solution.py:23
  364.6 5.5 %collective-permute-done.30 = bf16[2112,128]{1,0:T(8,128)(2,1)S(1)} collective-permute-done((bf16[2112,128]{1,0:T(8,128)(2,1)S(1)}, bf16[2112,128]{1,0:T(8,128)(2,1)S(1)}, u32[]{:S(2)}, u32[]{:S(2)}) %collective-permute-start.30) | collective-permute-done | bytes 540704 | tf_op jit(solution)/shard_map/ppermute | solution.py:23
  370.1 12.6 %collective-permute-done.32 = bf16[2112,128]{1,0:T(8,128)(2,1)S(1)} collective-permute-done((bf16[2112,128]{1,0:T(8,128)(2,1)S(1)}, bf16[2112,128]{1,0:T(8,128)(2,1)S(1)}, u32[]{:S(2)}, u32[]{:S(2)}) %collective-permute-start.32) | collective-permute-done | bytes 540704 | tf_op jit(solution)/shard_map/ppermute | solution.py:23
  386.8 5.9 %collective-permute-start.27 = (f32[256,100]{0,1:T(8,128)S(1)}, f32[256,100]{0,1:T(8,128)S(1)}, u32[]{:S(2)}, u32[]{:S(2)}) collective-permute-start(f32[256,100]{0,1:T(8,128)S(1)} %get-tuple-element.209), channel_id=1, source_target_pairs={{1,0},{0,1},{5,2},{4,3},{3,4},{2,5},{7,6},{6,7},{9,8},{8,9},{13,10... | collective-permute-start | bytes 307208 | tf_op jit(solution)/shard_map/ppermute | solution.py:58
  392.8 4.1 collective-permute-start.28
  400.4 4.8 %collective-permute-done.28 = f32[256,100]{0,1:T(8,128)S(1)} collective-permute-done((f32[256,100]{0,1:T(8,128)S(1)}, f32[256,100]{0,1:T(8,128)S(1)}, u32[]{:S(2)}, u32[]{:S(2)}) %collective-permute-start.28) | collective-permute-done | bytes 102432 | tf_op jit(solution)/shard_map/ppermute | solution.py:58
  (947 shorter events, 279.0 us)
Async XLA Ops:
  4.1 29.5 %collective-permute-start.6 = (bf16[512,128]{1,0:T(8,128)(2,1)S(1)}, bf16[512,128]{1,0:T(8,128)(2,1)S(1)}, u32[]{:S(2)}, u32[]{:S(2)}) collective-permute-start(bf16[512,128]{1,0:T(8,128)(2,1)S(1)} %bitcast.779), channel_id=1, source_target_pairs={{0,3},{1,2},{2,1},{3,0},{4,7},{5,6},{6,5},{7,4},{8,11},{9,10},{10,... | collective-permute-start | bytes 393224 | tf_op jit(solution)/shard_map/ppermute | solution.py:28
  8.3 25.3 %collective-permute-start.5 = (bf16[512,128]{1,0:T(8,128)(2,1)S(1)}, bf16[512,128]{1,0:T(8,128)(2,1)S(1)}, u32[]{:S(2)}, u32[]{:S(2)}) collective-permute-start(bf16[512,128]{1,0:T(8,128)(2,1)S(1)} %bitcast.780), channel_id=1, source_target_pairs={{0,2},{1,3},{2,0},{3,1},{4,6},{5,7},{6,4},{7,5},{8,10},{9,11},{10,... | collective-permute-start | bytes 393224 | tf_op jit(solution)/shard_map/ppermute | solution.py:28
  8.3 25.3 %collective-permute-start.4 = (bf16[512,128]{1,0:T(8,128)(2,1)S(1)}, bf16[512,128]{1,0:T(8,128)(2,1)S(1)}, u32[]{:S(2)}, u32[]{:S(2)}) collective-permute-start(bf16[512,128]{1,0:T(8,128)(2,1)S(1)} %bitcast.781), channel_id=1, source_target_pairs={{0,1},{1,0},{2,3},{3,2},{4,5},{5,4},{6,7},{7,6},{8,9},{9,8},{10,11... | collective-permute-start | bytes 393224 | tf_op jit(solution)/shard_map/ppermute | solution.py:28
  8.7 28.4 %collective-permute-start.2 = (s32[2,1024]{1,0:T(2,128)S(1)}, s32[2,1024]{1,0:T(2,128)}, u32[]{:S(2)}, u32[]{:S(2)}) collective-permute-start(s32[2,1024]{1,0:T(2,128)S(1)} %add_bitcast_fusion), channel_id=1, source_target_pairs={{0,4},{4,0},{8,12},{12,8},{16,20},{20,16},{24,28},{28,24},{1,5},{5... | collective-permute-start | bytes 24584 | tf_op jit(solution)/shard_map/ppermute | solution.py:23
  10.4 26.9 %collective-permute-start.14 = (bf16[512,128]{1,0:T(8,128)(2,1)S(1)}, bf16[512,128]{1,0:T(8,128)(2,1)S(1)}, u32[]{:S(2)}, u32[]{:S(2)}) collective-permute-start(bf16[512,128]{1,0:T(8,128)(2,1)S(1)} %bitcast.776), channel_id=1, source_target_pairs={{0,3},{1,2},{2,1},{3,0},{4,7},{5,6},{6,5},{7,4},{8,11},{9,10},{10,... | collective-permute-start | bytes 393224 | tf_op jit(solution)/shard_map/ppermute | solution.py:28
  36.3 19.8 %collective-permute-start.9 = (bf16[4,512,128]{2,1,0:T(8,128)(2,1)S(1)}, bf16[4,512,128]{2,1,0:T(8,128)(2,1)S(1)}, u32[]{:S(2)}, u32[]{:S(2)}) collective-permute-start(bf16[4,512,128]{2,1,0:T(8,128)(2,1)S(1)} %get-tuple-element.200), channel_id=1, source_target_pairs={{0,24},{4,28},{8,16},{12,20},{16,8},{20,12},{24,0},{28,4},{1,25},{... | collective-permute-start | bytes 1572872 | tf_op jit(solution)/shard_map/ppermute | solution.py:23
  42.4 42.0 %collective-permute-start = (f32[256,100]{0,1:T(8,128)}, f32[256,100]{0,1:T(8,128)S(1)}, u32[]{:S(2)}, u32[]{:S(2)}) collective-permute-start(f32[256,100]{0,1:T(8,128)} %get-tuple-element.211), channel_id=1, source_target_pairs={{0,1},{1,0},{2,5},{3,4},{4,3},{5,2},{6,7},{7,6},{8,9},{9,8},{10,13... | collective-permute-start | bytes 307208 | tf_op jit(solution)/shard_map/ppermute | solution.py:46
  49.7 24.3 %collective-permute-start.16 = (bf16[4,512,128]{2,1,0:T(8,128)(2,1)S(1)}, bf16[4,512,128]{2,1,0:T(8,128)(2,1)S(1)}, u32[]{:S(2)}, u32[]{:S(2)}) collective-permute-start(bf16[4,512,128]{2,1,0:T(8,128)(2,1)S(1)} %get-tuple-element.206), channel_id=1, source_target_pairs={{0,16},{4,20},{8,24},{12,28},{16,0},{20,4},{24,8},{28,12},{1,17},{... | collective-permute-start | bytes 1572872 | tf_op jit(solution)/shard_map/ppermute | solution.py:23
  51.0 24.9 %collective-permute-start.15 = (bf16[4,512,128]{2,1,0:T(8,128)(2,1)S(1)}, bf16[4,512,128]{2,1,0:T(8,128)(2,1)S(1)}, u32[]{:S(2)}, u32[]{:S(2)}) collective-permute-start(bf16[4,512,128]{2,1,0:T(8,128)(2,1)S(1)} %get-tuple-element.206), channel_id=1, source_target_pairs={{0,8},{4,12},{8,0},{12,4},{16,24},{20,28},{24,16},{28,20},{1,9},{5... | collective-permute-start | bytes 1572872 | tf_op jit(solution)/shard_map/ppermute | solution.py:23
  52.2 28.4 %collective-permute-start.17 = (bf16[4,512,128]{2,1,0:T(8,128)(2,1)S(1)}, bf16[4,512,128]{2,1,0:T(8,128)(2,1)S(1)}, u32[]{:S(2)}, u32[]{:S(2)}) collective-permute-start(bf16[4,512,128]{2,1,0:T(8,128)(2,1)S(1)} %get-tuple-element.206), channel_id=1, source_target_pairs={{0,24},{4,28},{8,16},{12,20},{16,8},{20,12},{24,0},{28,4},{1,25},{... | collective-permute-start | bytes 1572872 | tf_op jit(solution)/shard_map/ppermute | solution.py:23
  56.3 35.5 %collective-permute-start.10 = (bf16[4,4,512,128]{3,2,1,0:T(8,128)(2,1)S(1)}, bf16[4,4,512,128]{3,2,1,0:T(8,128)(2,1)S(1)}, u32[]{:S(2)}, u32[]{:S(2)}) collective-permute-start(bf16[4,4,512,128]{3,2,1,0:T(8,128)(2,1)S(1)} %pad_maximum_fusion.4), channel_id=1, source_target_pairs={{0,4},{4,0},{8,12},{12,8},{16,20},{20,16},{24,28},{28,24},{1,5},{5... | collective-permute-start | bytes 6291464 | tf_op jit(solution)/shard_map/ppermute | solution.py:23
  75.9 76.6 %collective-permute-start.23 = (bf16[256,512]{0,1:T(8,128)(2,1)}, bf16[256,512]{0,1:T(8,128)(2,1)S(1)}, u32[]{:S(2)}, u32[]{:S(2)}) collective-permute-start(bf16[256,512]{0,1:T(8,128)(2,1)} %get-tuple-element.193), channel_id=1, source_target_pairs={{0,0},{1,1},{2,4},{3,5},{4,2},{5,3},{6,6},{7,7},{8,8},{9,9},{10,12... | collective-permute-start | bytes 786440 | tf_op jit(solution)/shard_map/ppermute | solution.py:46
  80.6 71.9 %collective-permute-start.22 = (bf16[256,512]{0,1:T(8,128)(2,1)S(1)}, bf16[256,512]{0,1:T(8,128)(2,1)S(1)}, u32[]{:S(2)}, u32[]{:S(2)}) collective-permute-start(bf16[256,512]{0,1:T(8,128)(2,1)S(1)} %get-tuple-element.194), channel_id=1, source_target_pairs={{0,1},{1,0},{2,5},{3,4},{4,3},{5,2},{6,7},{7,6},{8,9},{9,8},{10,13... | collective-permute-start | bytes 786440 | tf_op jit(solution)/shard_map/ppermute | solution.py:46
  165.0 147.0 %collective-permute-start.20 = (bf16[256,512]{0,1:T(8,128)(2,1)}, bf16[256,512]{0,1:T(8,128)(2,1)}, u32[]{:S(2)}, u32[]{:S(2)}) collective-permute-start(bf16[256,512]{0,1:T(8,128)(2,1)} %get-tuple-element.197), channel_id=1, source_target_pairs={{1,0},{0,1},{5,2},{4,3},{3,4},{2,5},{7,6},{6,7},{9,8},{8,9},{13,10... | collective-permute-start | bytes 786440 | tf_op jit(solution)/shard_map/ppermute | solution.py:58
  165.0 148.1 %collective-permute-start.21 = (bf16[256,512]{0,1:T(8,128)(2,1)}, bf16[256,512]{0,1:T(8,128)(2,1)}, u32[]{:S(2)}, u32[]{:S(2)}) collective-permute-start(bf16[256,512]{0,1:T(8,128)(2,1)} %get-tuple-element.198), channel_id=1, source_target_pairs={{0,0},{1,1},{4,2},{5,3},{2,4},{3,5},{6,6},{7,7},{8,8},{9,9},{12,10... | collective-permute-start | bytes 786440 | tf_op jit(solution)/shard_map/ppermute | solution.py:58
  180.9 31.5 %collective-permute-start.24 = (bf16[512,1024]{0,1:T(8,128)(2,1)}, bf16[512,1024]{0,1:T(8,128)(2,1)}, u32[]{:S(2)}, u32[]{:S(2)}) collective-permute-start(bf16[512,1024]{0,1:T(8,128)(2,1)} %slice.1228), channel_id=1, source_target_pairs={{0,4},{4,0},{8,12},{12,8},{16,20},{20,16},{24,28},{28,24},{1,5},{5... | collective-permute-start | bytes 3145736 | tf_op jit(solution)/shard_map/ppermute | solution.py:23
  265.3 24.6 %collective-permute-start.25 = (bf16[512,1024]{0,1:T(8,128)(2,1)}, bf16[512,1024]{0,1:T(8,128)(2,1)}, u32[]{:S(2)}, u32[]{:S(2)}) collective-permute-start(bf16[512,1024]{0,1:T(8,128)(2,1)} %slice.1227), channel_id=1, source_target_pairs={{0,4},{4,0},{8,12},{12,8},{16,20},{20,16},{24,28},{28,24},{1,5},{5... | collective-permute-start | bytes 3145736 | tf_op jit(solution)/shard_map/ppermute | solution.py:23
  283.7 22.6 %collective-permute-start.40 = (bf16[4,2048,128]{2,1,0:T(8,128)(2,1)}, bf16[4,2048,128]{2,1,0:T(8,128)(2,1)}, u32[]{:S(2)}, u32[]{:S(2)}) collective-permute-start(bf16[4,2048,128]{2,1,0:T(8,128)(2,1)} %dynamic-slice_bitcast_fusion), channel_id=1, source_target_pairs={{0,4},{4,0},{8,12},{12,8},{16,20},{20,16},{24,28},{28,24},{1,5},{5... | collective-permute-start | bytes 6291464 | tf_op jit(solution)/shard_map/ppermute | solution.py:23
  306.1 48.5 %collective-permute-start.29 = (bf16[4,2112,128]{2,1,0:T(8,128)(2,1)}, bf16[4,2112,128]{2,1,0:T(8,128)(2,1)}, u32[]{:S(2)}, u32[]{:S(2)}) collective-permute-start(bf16[4,2112,128]{2,1,0:T(8,128)(2,1)} %fusion.3), channel_id=1, source_target_pairs={{0,4},{4,0},{8,12},{12,8},{16,20},{20,16},{24,28},{28,24},{1,5},{5... | collective-permute-start | bytes 6488072 | tf_op jit(solution)/shard_map/ppermute | solution.py:23
  311.9 24.6 %collective-permute-start.43 = (bf16[2048,128]{1,0:T(8,128)(2,1)}, bf16[2048,128]{1,0:T(8,128)(2,1)}, u32[]{:S(2)}, u32[]{:S(2)}) collective-permute-start(bf16[2048,128]{1,0:T(8,128)(2,1)} %get-tuple-element.110), channel_id=1, source_target_pairs={{0,24},{4,28},{8,16},{12,20},{16,8},{20,12},{24,0},{28,4},{1,25},{... | collective-permute-start | bytes 1572872 | tf_op jit(solution)/shard_map/ppermute | solution.py:23
  313.1 24.2 %collective-permute-start.42 = (bf16[2048,128]{1,0:T(8,128)(2,1)}, bf16[2048,128]{1,0:T(8,128)(2,1)}, u32[]{:S(2)}, u32[]{:S(2)}) collective-permute-start(bf16[2048,128]{1,0:T(8,128)(2,1)} %get-tuple-element.111), channel_id=1, source_target_pairs={{0,16},{4,20},{8,24},{12,28},{16,0},{20,4},{24,8},{28,12},{1,17},{... | collective-permute-start | bytes 1572872 | tf_op jit(solution)/shard_map/ppermute | solution.py:23
  358.2 24.6 %collective-permute-start.32 = (bf16[2112,128]{1,0:T(8,128)(2,1)S(1)}, bf16[2112,128]{1,0:T(8,128)(2,1)S(1)}, u32[]{:S(2)}, u32[]{:S(2)}) collective-permute-start(bf16[2112,128]{1,0:T(8,128)(2,1)S(1)} %get-tuple-element.103), channel_id=1, source_target_pairs={{0,24},{4,28},{8,16},{12,20},{16,8},{20,12},{24,0},{28,4},{1,25},{... | collective-permute-start | bytes 1622024 | tf_op jit(solution)/shard_map/ppermute | solution.py:23
  358.4 24.4 %collective-permute-start.31 = (bf16[2112,128]{1,0:T(8,128)(2,1)S(1)}, bf16[2112,128]{1,0:T(8,128)(2,1)S(1)}, u32[]{:S(2)}, u32[]{:S(2)}) collective-permute-start(bf16[2112,128]{1,0:T(8,128)(2,1)S(1)} %get-tuple-element.104), channel_id=1, source_target_pairs={{0,16},{4,20},{8,24},{12,28},{16,0},{20,4},{24,8},{28,12},{1,17},{... | collective-permute-start | bytes 1622024 | tf_op jit(solution)/shard_map/ppermute | solution.py:23
  359.9 46.2 %collective-permute-start.50 = (bf16[4,512,128]{2,1,0:T(8,128)(2,1)S(1)}, bf16[4,512,128]{2,1,0:T(8,128)(2,1)S(1)}, u32[]{:S(2)}, u32[]{:S(2)}) collective-permute-start(bf16[4,512,128]{2,1,0:T(8,128)(2,1)S(1)} %bitcast.685), channel_id=1, source_target_pairs={{0,4},{4,0},{8,12},{12,8},{16,20},{20,16},{24,28},{28,24},{1,5},{5... | collective-permute-start | bytes 1572872 | tf_op jit(solution)/shard_map/ppermute | solution.py:23
  (234 other events, 1305.6 us)
